TPU v7x, 32 devices: a whole 2x2x4 slice. The times are simulated.
32 devices in a mesh: expert: 16 (over z, x, core), tensor: 2 (over y), dp: 1.
Axes of the slice: x: 2, y: 2, z: 4, core: 2. Of those that a mesh axis runs over, the one named last changes fastest.
Arguments:
- tokens: bfloat16 [1536, 5120], P(('dp', 'expert'), 'tensor'), may hold values from -6 to 6
- routes: int32 [1536, 6], P(('dp', 'expert')), may hold values from 0 to 15, all different within a row; in each aligned block of 96 rows (0 to 95, 96 to 191, ...) at most 36 rows name the same one
- gates: float32 [1536, 6], P(('dp', 'expert')), may hold values from 0.05 to 0.6
- gate_up: bfloat16 [16, 5120, 2, 1024], P('expert', None, None, 'tensor'), may hold values from -0.078125 to 0.078125
- down_weight: bfloat16 [16, 5120, 1024], P('expert', None, 'tensor'), may hold values from -0.1875 to 0.1875
- old_map: int32 [16], replicated, may hold values from 0 to 15, each once
- new_map: int32 [16], replicated, may hold values from 0 to 15, each once
Outputs:
- mixed: bfloat16 [1536, 5120], P(('dp', 'expert'), 'tensor')
Inputs may be any that keep to these rules, and one draw needn't show every extreme that they name: `routes`: each row names 6 different slots; in each aligned block of 96 rows (the rows of one index of expert) no slot is named by more than 36 rows; since each row names 6 different slots, every slot is then named by exactly 36 rows of every block. `old_map`: each expert appears exactly once. `new_map`: each expert appears exactly once.
All inputs are finite; a program needn't handle non-finite values.
Results may differ from a plain program's by a relative error of at most 0.0058.
Values may be sent and summed in bfloat16 or wider, within the bound.
A program may use at most 128 MiB of HBM per device.

v0:
```python
import jax
import jax.numpy as jnp
from jax import lax
from jax.sharding import PartitionSpec as P


def local(tokens, routes, gates, gate_up, down_weight, old_map, new_map):
    experts = lax.axis_size("expert")
    tensor_count = lax.axis_size("tensor")
    tok_rows = tokens.shape[0]
    feature_part = tokens.shape[1]
    picks_row = routes.shape[1]
    capacity = (tok_rows * picks_row + experts - 1) // experts
    width = gate_up.shape[1]
    hidden = down_weight.shape[2]
    buffer_rows = experts * capacity
    slot_ids = jnp.arange(experts, dtype=jnp.int32)
    holder = jnp.sum(jnp.where(new_map[:, None] == old_map[None, :], slot_ids[None, :], 0), axis=1)
    weight_in = gate_up.reshape(width, 2 * hidden)
    weight_out = down_weight.reshape(width, hidden)
    target = jnp.sum(
        jnp.where(routes[:, :, None] == slot_ids[None, None, :], holder[None, None, :], 0), axis=2
    )
    flat_target = target.reshape(-1)
    onehot = (flat_target[:, None] == slot_ids[None, :]).astype(jnp.int32)
    earlier = jnp.cumsum(onehot, axis=0) - onehot
    position = jnp.sum(earlier * onehot, axis=1)
    slot_index = flat_target * capacity + position
    columns = jnp.arange(buffer_rows, dtype=jnp.int32)
    matches = (slot_index[:, None] == columns[None, :]).reshape(tok_rows, picks_row, buffer_rows)
    assign = jnp.sum(matches.astype(jnp.float32), axis=1).astype(jnp.bfloat16)
    combine_weights = jnp.sum(jnp.where(matches, gates[:, :, None], 0.0), axis=1)
    outgoing = lax.dot_general(
        assign, tokens, (((0,), (0,)), ((), ())), preferred_element_type=jnp.float32
    )
    outgoing = outgoing.astype(jnp.bfloat16).reshape(experts, capacity, feature_part)
    arrived = lax.all_to_all(outgoing, "expert", split_axis=0, concat_axis=0, tiled=True)
    piece = lax.all_gather(arrived, "tensor", axis=2, tiled=True)
    flat_piece = piece.reshape(buffer_rows, piece.shape[2])
    projected = jnp.dot(flat_piece, weight_in, preferred_element_type=jnp.float32)
    activation = (jax.nn.silu(projected[:, :hidden]) * projected[:, hidden:]).astype(jnp.bfloat16)
    down_parts = weight_out.reshape(tensor_count, width // tensor_count, hidden)
    down_mine = lax.all_to_all(
        down_parts, "tensor", split_axis=0, concat_axis=2, tiled=True
    ).reshape(width // tensor_count, tensor_count * hidden)
    summed = lax.dot_general(
        lax.all_gather(activation, "tensor", axis=1, tiled=True),
        down_mine,
        (((1,), (1,)), ((), ())),
        preferred_element_type=jnp.float32,
    )
    expert_out = summed.astype(jnp.bfloat16).reshape(experts, capacity, feature_part)
    returned = lax.all_to_all(expert_out, "expert", split_axis=0, concat_axis=0, tiled=True)
    gathered_back = returned.reshape(buffer_rows, feature_part).astype(jnp.float32)
    mixed = jnp.dot(
        combine_weights,
        gathered_back,
        precision=lax.Precision.HIGHEST,
        preferred_element_type=jnp.float32,
    )
    return mixed.astype(jnp.bfloat16)


def solution(mesh):
    in_specs = (
        P(("dp", "expert"), "tensor"),
        P(("dp", "expert"), None),
        P(("dp", "expert"), None),
        P("expert", None, None, "tensor"),
        P("expert", None, "tensor"),
        P(),
        P(),
    )
    out_specs = P(("dp", "expert"), "tensor")
    return jax.shard_map(local, mesh=mesh, in_specs=in_specs, out_specs=out_specs, check_vma=False)
```

profile of v0, /device:TPU:0, one launch (start us, length us, event | category | flops | bytes accessed | tf_op | source)
XLA Modules:
  0.0 379.6 jit_solution(490913484505639528)
XLA Ops:
  6.5 0.0 copy-start
  6.5 0.0 all-gather.3.cloned.1.call-start
  6.5 0.9 select_reduce_fusion.2
  7.4 0.8 select_reduce_fusion.1
  8.2 0.1 copy.19
  8.3 0.1 eq.68
  8.5 1.4 reduce-window.6
  9.9 0.2 slice_reduce_fusion
  10.2 0.1 bitcast_bitcast_fusion
  10.3 0.1 reduce_sum.50
  10.5 0.1 copy.22
  10.5 1.8 convert_reduce_fusion
  12.3 0.0 copy-done
  12.3 2.5 convolution_convert_fusion
  14.8 2.8 reshape.56
  17.7 81.7 %all_to_all.25 = bf16[16,36,2560]{2,1,0:T(8,128)(2,1)} all-to-all(bf16[16,36,2560]{2,1,0:T(8,128)(2,1)S(1)} %reshape.56), channel_id=1, replica_groups=mesh['expert'=16,'tensor'=2,'dp'=1] {'expert'}, dimensions={0} | all-to-all | bytes 5898240 | tf_op jit(solution)/shard_map/all_to_all | solution.py:37
  99.4 0.0 all-gather.3.cloned.1.call-update
  99.4 6.0 %all-to-all-start.1 = ((bf16[2,2560,512]{2,1,0:T(8,128)(2,1)}), bf16[2,2560,512]{2,1,0:T(8,128)(2,1)}, u32[]{:S(2)}, u32[]{:S(2)}) async-start(bf16[2,2560,512]{2,1,0:T(8,128)(2,1)} %bitcast.31), calls=%async_computation.1 | async-start | bytes 10485760 | tf_op jit(solution)/shard_map/all_to_all | solution.py:43
  105.4 0.0 all-gather.5.cloned.1.call-start
  105.4 12.9 %copy.26 = bf16[640,8,2,512]{3,1,2,0:T(8,128)(2,1)} copy(bf16[640,8,2,512]{3,2,1,0:T(2,128)(2,1)} %bitcast.29) | data formatting | bytes 20971520
  118.3 116.8 %all-gather.3.cloned.1.call-done = bf16[16,36,5120]{2,1,0:T(8,128)(2,1)} async-done(((bf16[16,36,2560]{2,1,0:T(8,128)(2,1)}), bf16[16,36,5120]{2,1,0:T(8,128)(2,1)}) %all-gather.3.cloned.1.call-update) | async-done | bytes 5898256 | tf_op jit(solution)/shard_map/all_gather | solution.py:38
  235.1 8.2 %reshape.57 = bf16[576,5120]{1,0:T(8,128)(2,1)} reshape(bf16[16,36,5120]{2,1,0:T(8,128)(2,1)} %all-gather.3.cloned.1.call-done) | data formatting | bytes 11796480 | tf_op jit(solution)/shard_map/reshape | solution.py:39
  243.3 10.7 %fusion.4 = f32[576,1024]{1,0:T(8,128)S(1)} fusion(bf16[576,5120]{1,0:T(8,128)(2,1)} %reshape.57, bf16[5120,1024]{1,0:T(8,128)(2,1)} %bitcast.30), kind=kOutput, calls=%fused_computation.23 | convolution fusion | flops 6039797760 | bytes 18743296 | tf_op jit(solution)/shard_map/dot_general | solution.py:40
  254.0 1.2 fusion
  255.2 0.0 all-gather.5.cloned.1.call-update
  255.2 0.0 all-to-all-done.1
  255.2 8.0 %copy.23 = bf16[1,2560,2,512]{1,3,2,0:T(8,128)(2,1)} copy(bf16[1,2560,2,512]{3,1,2,0:T(8,128)(2,1)} %bitcast.3) | data formatting | bytes 10485760 | tf_op jit(solution)/shard_map/all_to_all | solution.py:43
  263.2 12.7 %all-gather.5.cloned.1.call-done = bf16[576,1024]{1,0:T(8,128)(2,1)} async-done(((bf16[576,512]{1,0:T(8,128)(2,1)}), bf16[576,1024]{1,0:T(8,128)(2,1)}) %all-gather.5.cloned.1.call-update) | async-done | bytes 1179664 | tf_op jit(solution)/shard_map/all_gather | solution.py:47
  275.9 7.6 %convolution_convert_fusion.1 = bf16[576,2560]{1,0:T(8,128)(2,1)} fusion(bf16[576,1024]{1,0:T(8,128)(2,1)} %all-gather.5.cloned.1.call-done, bf16[2560,1024]{0,1:T(8,128)(2,1)} %bitcast.32), kind=kOutput, calls=%fused_computation.1 | convolution fusion | flops 3021373440 | bytes 9371648 | tf_op jit(solution)/shard_map/dot_general | solution.py:46
  283.5 2.8 reshape.60
  286.4 79.9 %all_to_all.26 = bf16[16,36,2560]{2,1,0:T(8,128)(2,1)} all-to-all(bf16[16,36,2560]{2,1,0:T(8,128)(2,1)S(1)} %reshape.60), channel_id=1, replica_groups=mesh['expert'=16,'tensor'=2,'dp'=1] {'expert'}, dimensions={0} | all-to-all | bytes 5898240 | tf_op jit(solution)/shard_map/all_to_all | solution.py:53
  366.3 0.0 copy-start.1
  366.3 3.0 reshape.61
  369.3 3.5 convolution_convert_fusion.2
  372.8 0.0 copy-done.1
  (5 shorter events, 0.1 us)
Async XLA Ops:
  6.5 5.8 %copy-start = (bf16[96,2560]{1,0:T(8,128)(2,1)S(1)}, bf16[96,2560]{1,0:T(8,128)(2,1)}, u32[]{:S(2)}) copy-start(bf16[96,2560]{1,0:T(8,128)(2,1)} %param.7) | copy-start | bytes 1474564
  6.5 228.6 %all-gather.3.cloned.1.call-start = ((), (), s32[]{:S(2)}) async-start(), calls=%async_computation.3 | async-start | bytes 9830400 | tf_op jit(solution)/shard_map/all_gather | solution.py:38
  99.4 155.8 %all-to-all-start.1 = ((bf16[2,2560,512]{2,1,0:T(8,128)(2,1)}), bf16[2,2560,512]{2,1,0:T(8,128)(2,1)}, u32[]{:S(2)}, u32[]{:S(2)}) async-start(bf16[2,2560,512]{2,1,0:T(8,128)(2,1)} %bitcast.31), calls=%async_computation.1 | async-start | bytes 10485760 | tf_op jit(solution)/shard_map/all_to_all | solution.py:43
  105.4 170.5 %all-gather.5.cloned.1.call-start = ((), (), s32[]{:S(2)}) async-start(), calls=%async_computation.4 | async-start | bytes 1769472 | tf_op jit(solution)/shard_map/all_gather | solution.py:47
  366.3 6.5 %copy-start.1 = (bf16[96,2560]{1,0:T(8,128)(2,1)S(1)}, bf16[96,2560]{1,0:T(8,128)(2,1)}, u32[]{:S(2)}) copy-start(bf16[96,2560]{1,0:T(8,128)(2,1)} %param.7) | copy-start | bytes 1474564
Sparse Core Ops, SparseCore 0:
  99.5 135.5 all-gather.2
  255.3 20.5 all-gather.4
where the time goes:
time: 380 us
  blocking collectives  162 us (43%)
  waiting for transfers between devices  130 us (34%)
  local copies, waits for them, and re-layouts  38.2 us (10%)
  matrix products  24.3 us (6%)
  between operations  13.5 us (4%)
  other arithmetic  6.24 us (2%)
  starting transfers between devices  6.04 us (2%)
    all_gather x1, waiting for transfers between devices, local(): piece = lax.all_gather(arrived, 'tensor', axis=2, tiled=True)  117 us
    all_to_all x1, blocking collectives, local(): lax.all_to_all(outgoing, 'expert', split_axis=0, concat_axis=0, tiled=True)  81.7 us
    all_to_all x1, blocking collectives, local(): lax.all_to_all(expert_out, 'expert', split_axis=0, concat_axis=0, tiled=T...  79.9 us
    unnamed x5, local copies, waits for them, and re-layouts  12.9 us
    all_gather x1, waiting for transfers between devices, local(): lax.all_gather(activation, 'tensor', axis=1, tiled=True)  12.7 us
    dot_general x1, matrix products, local(): jnp.dot(flat_piece, weight_in, preferred_element_type=jnp.float32)  10.7 us
    reshape x1, local copies, waits for them, and re-layouts, local(): flat_piece = piece.reshape(buffer_rows, piece.shape[2])  8.17 us
    all_to_all x1, local copies, waits for them, and re-layouts, local(): lax.all_to_all(down_parts, 'tensor', split_axis=0, concat_axis=2, tiled=T...  7.96 us
  transfers between devices with their start and end apart: 3, of which 2 were waited for; matrix products, arithmetic and copies ran while one was open for 11% of the time, Pallas kernels for 0%

commit v1 on v0

v1 whole, which is shorter than its diff:
```python
import functools

import jax
import jax.numpy as jnp
from jax import lax
from jax.experimental import pallas as pl
from jax.experimental.pallas import tpu as pltpu
from jax.sharding import PartitionSpec as P

MESH = pl.DeviceIdType.MESH
VMEM_BUDGET = 56 * 2**20


def place(zs):
    e, y = lax.axis_index("expert"), lax.axis_index("tensor")
    z, x, c = lax.div(e, 4), lax.rem(lax.div(e, 2), 2), lax.rem(e, 2)
    return z, x, y, c


def device(z, x, y, c):
    return {"expert": (z * 2 + x) * 2 + c, "tensor": y}


def greet(zs, z, x, y, c):
    barrier = pltpu.get_barrier_semaphore()

    def hello(dev):
        pl.semaphore_signal(barrier, inc=1, device_id=dev, device_id_type=MESH)

    hello(device(z, 1 - x, y, c))
    hello(device(z, x, 1 - y, c))
    hello(device(z, x, y, 1 - c))
    pl.when(z > 0)(lambda: hello(device(z - 1, x, y, c)))
    pl.when(z < zs - 1)(lambda: hello(device(z + 1, x, y, c)))
    pl.semaphore_wait(barrier, 3 + (z > 0).astype(jnp.int32) + (z < zs - 1).astype(jnp.int32))


UP, DOWN, XL, YL, SIB = range(5)


def gather_kernel(zs, rows, tok_ref, out_ref, local_sem, send_sem, recv_sem):
    z, x, y, c = place(zs)
    half = rows // 2
    greet(zs, z, x, y, c)

    def slot(pz, px, py, pc, h):
        return out_ref.at[py, pl.ds(((pz * 2 + px) * 2 + pc) * rows + h * half, half), :]

    def index(pz, px, py):
        return (pz * 2 + px) * 2 + py

    def copy(link, pz, px, py, h, own=False):
        dev = (
            device(z + 1, x, y, c),
            device(z - 1, x, y, c),
            device(z, 1 - x, y, c),
            device(z, x, 1 - y, c),
            device(z, x, y, 1 - c),
        )[link]
        src = tok_ref.at[pl.ds(h * half, half), :] if own else slot(pz, px, py, c, h)
        i = index(pz, px, py)
        return pltpu.make_async_remote_copy(
            src_ref=src,
            dst_ref=slot(pz, px, py, c, h),
            send_sem=send_sem.at[link, i, h],
            recv_sem=recv_sem.at[c, i, h],
            device_id=dev,
            device_id_type=MESH,
        )

    def arrived(pz, px, py, pc, h):
        pltpu.make_async_copy(
            slot(pz, px, py, pc, h), slot(pz, px, py, pc, h), recv_sem.at[pc, index(pz, px, py), h]
        ).wait()

    def hop(d, fu, fv, h, act):
        pz = z + d
        px = 1 - x if (fu if h == 0 else fv) else x
        py = 1 - y if (fv if h == 0 else fu) else y
        u, v = (XL, YL) if h == 0 else (YL, XL)
        own = d == 0 and not fu and not fv
        if not fu and not fv:
            if d <= 0:
                pl.when(z < zs - 1)(lambda: act(copy(UP, pz, px, py, h, own)))
            if d >= 0:
                pl.when(z > 0)(lambda: act(copy(DOWN, pz, px, py, h, own)))
        if not fu and not fv:
            act(copy(u, pz, px, py, h, own))
        if not fv:
            act(copy(v, pz, px, py, h, own))
        act(copy(SIB, pz, px, py, h, own))

    events = [
        (d, fu, fv, h)
        for d in range(-(zs - 1), zs)
        for fu in (0, 1)
        for fv in (0, 1)
        for h in (0, 1)
    ]
    events.sort(key=lambda t: (abs(t[0]) + t[1] + t[2], t[2], t[1]))
    mine = pltpu.make_async_copy(
        tok_ref, out_ref.at[y, pl.ds(((z * 2 + x) * 2 + c) * rows, rows), :], local_sem
    )
    mine.start()
    for d, fu, fv, h in events:

        def step(d=d, fu=fu, fv=fv, h=h):
            if d or fu or fv:
                px = 1 - x if (fu if h == 0 else fv) else x
                py = 1 - y if (fv if h == 0 else fu) else y
                arrived(z + d, px, py, c, h)
            hop(d, fu, fv, h, lambda k: k.start())

        if d == 0:
            step()
        else:
            pl.when((z + d >= 0) & (z + d < zs))(step)
    mine.wait()
    for pz in range(zs):
        for px in range(2):
            for py in range(2):
                for h in range(2):
                    arrived(pz, px, py, 1 - c, h)
    for d, fu, fv, h in events:

        def finish(d=d, fu=fu, fv=fv, h=h):
            hop(d, fu, fv, h, lambda k: k.wait_send())

        if d == 0:
            finish()
        else:
            pl.when((z + d >= 0) & (z + d < zs))(finish)


def scatter_kernel(zs, rows, part_ref, out_ref, acc, rv, ru, rz, send_sem, sib_sem, v_sem, u_sem, z_sem):
    z, x, y, c = place(zs)
    half = rows // 2
    greet(zs, z, x, y, c)

    def index(pz, px, py):
        return (pz * 2 + px) * 2 + py

    def mine(pz, px, py, pc, h):
        return part_ref.at[py, pl.ds(((pz * 2 + px) * 2 + pc) * rows + h * half, half), :]

    def spot(d, fu, fv, h):
        return z + d, (1 - x if (fu if h == 0 else fv) else x), (1 - y if (fv if h == 0 else fu) else y)

    def add(dst, *srcs):
        def body(i, _):
            r = pl.ds(pl.multiple_of(i * 16, 16), 16)
            total = srcs[0][r, :].astype(jnp.float32)
            for s in srcs[1:]:
                total = total + s[r, :].astype(jnp.float32)
            dst[r, :] = total.astype(dst.dtype)
            return 0

        lax.fori_loop(0, half // 16, body, 0)

    def sib_copy(pz, px, py, h):
        i = index(pz, px, py)
        return pltpu.make_async_remote_copy(
            src_ref=mine(pz, px, py, 1 - c, h),
            dst_ref=acc.at[i, h],
            send_sem=send_sem.at[0, i, h],
            recv_sem=sib_sem.at[i, h],
            device_id=device(z, x, y, 1 - c),
            device_id_type=MESH,
        )

    def v_copy(d, fu, h):
        pz, px, py = spot(d, fu, 1, h)
        i = index(pz, px, py)
        dev = device(z, x, 1 - y, c) if h == 0 else device(z, 1 - x, y, c)
        k = pz * 2 + (px if h == 0 else py)
        return pltpu.make_async_remote_copy(
            src_ref=acc.at[i, h],
            dst_ref=rv.at[k, h],
            send_sem=send_sem.at[1, i, h],
            recv_sem=v_sem.at[k, h],
            device_id=dev,
            device_id_type=MESH,
        )

    def u_copy(d, h):
        pz, px, py = spot(d, 1, 0, h)
        i = index(pz, px, py)
        dev = device(z, 1 - x, y, c) if h == 0 else device(z, x, 1 - y, c)
        return pltpu.make_async_remote_copy(
            src_ref=acc.at[i, h],
            dst_ref=ru.at[pz, h],
            send_sem=send_sem.at[2, i, h],
            recv_sem=u_sem.at[pz, h],
            device_id=dev,
            device_id_type=MESH,
        )

    def z_copy(d, h):
        pz, px, py = spot(d, 0, 0, h)
        i = index(pz, px, py)
        way = 0 if d > 0 else 1
        return pltpu.make_async_remote_copy(
            src_ref=acc.at[i, h],
            dst_ref=rz.at[way, pz, h],
            send_sem=send_sem.at[3, i, h],
            recv_sem=z_sem.at[way, pz, h],
            device_id=device(z + 1 if d > 0 else z - 1, x, y, c),
            device_id_type=MESH,
        )

    def landed(ref, sem):
        pltpu.make_async_copy(ref, ref, sem).wait()

    def when_there(d, f):
        if d == 0:
            f()
        else:
            pl.when((z + d >= 0) & (z + d < zs))(f)

    order = [[s * k for s in ((1, -1) if k else (1,))] for k in range(zs - 1, -1, -1)]
    pairs = [(fu, fv) for fv in (1, 0) for fu in (1, 0)]

    def first(ds):
        for d in ds:
            for fu, fv in pairs:
                for h in (0, 1):
                    when_there(d, lambda: sib_copy(*spot(d, fu, fv, h), h).start())

    def stage0(ds):
        for d in ds:

            def run():
                for fu, fv in pairs:
                    for h in (0, 1):
                        pz, px, py = spot(d, fu, fv, h)
                        i = index(pz, px, py)
                        landed(acc.at[i, h], sib_sem.at[i, h])
                        add(acc.at[i, h], acc.at[i, h], mine(pz, px, py, c, h))
                        if fv:
                            v_copy(d, fu, h).start()

            when_there(d, run)

    def stage1(ds):
        for d in ds:

            def run():
                for fu in (1, 0):
                    for h in (0, 1):
                        pz, px, py = spot(d, fu, 0, h)
                        i = index(pz, px, py)
                        k = pz * 2 + (px if h == 0 else py)
                        landed(rv.at[k, h], v_sem.at[k, h])
                        add(acc.at[i, h], acc.at[i, h], rv.at[k, h])
                        if fu:
                            u_copy(d, h).start()

            when_there(d, run)

    def stage2(ds):
        for d in ds:

            def run():
                for h in (0, 1):
                    pz, px, py = spot(d, 0, 0, h)
                    i = index(pz, px, py)
                    landed(ru.at[pz, h], u_sem.at[pz, h])
                    add(acc.at[i, h], acc.at[i, h], ru.at[pz, h])
                    for way, source in ((0, z > 0), (1, z < zs - 1)):
                        if (way == 0 and d < 0) or (way == 1 and d > 0):
                            continue

                        def more():
                            landed(rz.at[way, pz, h], z_sem.at[way, pz, h])
                            add(acc.at[i, h], acc.at[i, h], rz.at[way, pz, h])

                        pl.when(source)(more)
                    if d:
                        z_copy(d, h).start()
                    else:
                        add(out_ref.at[pl.ds(h * half, half), :], acc.at[i, h])

            when_there(d, run)

    for ds in order:
        first(ds)
    n = len(order)
    for t in range(n + 2):
        if t < n:
            stage0(order[t])
        if 0 <= t - 1 < n:
            stage1(order[t - 1])
        if 0 <= t - 2 < n:
            stage2(order[t - 2])
    for ds in order:
        for d in ds:

            def done():
                for h in (0, 1):
                    for fu, fv in pairs:
                        sib_copy(*spot(d, fu, fv, h), h).wait_send()
                    for fu in (0, 1):
                        v_copy(d, fu, h).wait_send()
                    u_copy(d, h).wait_send()
                    if d:
                        z_copy(d, h).wait_send()

            when_there(d, done)


def weights_of(routes, gates, old_map, new_map):
    experts = lax.axis_size("expert")
    ids = jnp.arange(experts, dtype=jnp.int32)
    holder = jnp.sum(jnp.where(new_map[:, None] == old_map[None, :], ids[None, :], 0), axis=1)
    target = jnp.sum(jnp.where(routes[:, :, None] == ids, holder, 0), axis=2)
    return jnp.sum(jnp.where(target[:, :, None] == ids, gates[:, :, None], 0.0), axis=1)


def gathered(tokens, routes, gates, gate_up, down_weight, old_map, new_map):
    experts, tensors = lax.axis_size("expert"), lax.axis_size("tensor")
    zs = experts // 4
    rows, part = tokens.shape
    _, width, _, hidden = gate_up.shape
    dma = pltpu.SemaphoreType.DMA
    mine = lax.axis_index("expert")
    table = lax.all_gather(
        weights_of(routes, gates, old_map, new_map).T, "expert", axis=1, tiled=True
    )
    share = lax.dynamic_index_in_dim(table, mine, 0, keepdims=False)[:, None]
    every = pl.pallas_call(
        functools.partial(gather_kernel, zs, rows),
        out_shape=jax.ShapeDtypeStruct((tensors, experts * rows, part), tokens.dtype),
        in_specs=[pl.BlockSpec(memory_space=pl.ANY)],
        out_specs=pl.BlockSpec(memory_space=pl.ANY),
        scratch_shapes=[dma, dma((5, zs * 4, 2)), dma((2, zs * 4, 2))],
        compiler_params=pltpu.CompilerParams(
            collective_id=0, has_side_effects=True, vmem_limit_bytes=VMEM_BUDGET
        ),
        name="gather_tokens",
    )(tokens)
    w_in = gate_up.reshape(width, 2 * hidden)
    projected = sum(
        jnp.dot(every[k], w_in[k * part : (k + 1) * part], preferred_element_type=jnp.float32)
        for k in range(tensors)
    )
    act = (jax.nn.silu(projected[:, :hidden]) * projected[:, hidden:]).astype(jnp.bfloat16)
    w_out = down_weight.reshape(tensors, part, hidden)
    partial = jnp.stack(
        [
            (
                share
                * lax.dot_general(
                    act, w_out[k], (((1,), (1,)), ((), ())), preferred_element_type=jnp.float32
                )
            ).astype(jnp.bfloat16)
            for k in range(tensors)
        ]
    )
    half = rows // 2
    return pl.pallas_call(
        functools.partial(scatter_kernel, zs, rows),
        out_shape=jax.ShapeDtypeStruct((rows, part), jnp.bfloat16),
        in_specs=[pl.BlockSpec(memory_space=pltpu.VMEM)],
        out_specs=pl.BlockSpec(memory_space=pltpu.VMEM),
        scratch_shapes=[
            pltpu.VMEM((zs * 4, 2, half, part), jnp.bfloat16),
            pltpu.VMEM((zs * 2, 2, half, part), jnp.bfloat16),
            pltpu.VMEM((zs, 2, half, part), jnp.bfloat16),
            pltpu.VMEM((2, zs, 2, half, part), jnp.bfloat16),
            dma((4, zs * 4, 2)),
            dma((zs * 4, 2)),
            dma((zs * 2, 2)),
            dma((zs, 2)),
            dma((2, zs, 2)),
        ],
        compiler_params=pltpu.CompilerParams(
            collective_id=1, has_side_effects=True, vmem_limit_bytes=VMEM_BUDGET
        ),
        name="scatter_sums",
    )(partial)


def routed(tokens, routes, gates, gate_up, down_weight, old_map, new_map):
    experts, tensors = lax.axis_size("expert"), lax.axis_size("tensor")
    rows, part = tokens.shape
    picks = routes.shape[1]
    capacity = (rows * picks + experts - 1) // experts
    _, width, _, hidden = gate_up.shape
    total = experts * capacity
    weight = weights_of(routes, gates, old_map, new_map)
    chosen = weights_of(routes, jnp.ones_like(gates), old_map, new_map)
    earlier = jnp.tril(jnp.ones((rows, rows), jnp.bfloat16), -1)
    position = jnp.dot(
        earlier, chosen.astype(jnp.bfloat16), preferred_element_type=jnp.float32
    ).astype(jnp.int32)
    hit = (position[:, :, None] == jnp.arange(capacity)) & (chosen[:, :, None] > 0)
    assign = hit.astype(jnp.bfloat16).reshape(rows, total)
    combine = jnp.where(hit, weight[:, :, None], 0.0).reshape(rows, total)
    outgoing = lax.dot_general(
        assign, tokens, (((0,), (0,)), ((), ())), preferred_element_type=jnp.float32
    )
    outgoing = outgoing.astype(jnp.bfloat16).reshape(experts, capacity, part)
    arrived = lax.all_to_all(outgoing, "expert", split_axis=0, concat_axis=0, tiled=True)
    piece = lax.all_gather(arrived, "tensor", axis=2, tiled=True).reshape(total, width)
    projected = jnp.dot(
        piece, gate_up.reshape(width, 2 * hidden), preferred_element_type=jnp.float32
    )
    act = (jax.nn.silu(projected[:, :hidden]) * projected[:, hidden:]).astype(jnp.bfloat16)
    down = lax.all_to_all(
        down_weight.reshape(tensors, part, hidden), "tensor", split_axis=0, concat_axis=2, tiled=True
    ).reshape(part, tensors * hidden)
    out = lax.dot_general(
        lax.all_gather(act, "tensor", axis=1, tiled=True),
        down,
        (((1,), (1,)), ((), ())),
        preferred_element_type=jnp.float32,
    )
    out = out.astype(jnp.bfloat16).reshape(experts, capacity, part)
    back = lax.all_to_all(out, "expert", split_axis=0, concat_axis=0, tiled=True)
    mixed = jnp.dot(
        combine,
        back.reshape(total, part).astype(jnp.float32),
        precision=lax.Precision.HIGHEST,
        preferred_element_type=jnp.float32,
    )
    return mixed.astype(jnp.bfloat16)


def local(*args):
    experts, tensors = lax.axis_size("expert"), lax.axis_size("tensor")
    rows, part = args[0].shape
    held = experts * rows * part * 2 * (tensors + 2)
    fits = tensors == 2 and experts % 4 == 0 and experts >= 8 and rows % 32 == 0
    if fits and held < VMEM_BUDGET:
        return gathered(*args)
    return routed(*args)


def solution(mesh):
    in_specs = (
        P(("dp", "expert"), "tensor"),
        P(("dp", "expert"), None),
        P(("dp", "expert"), None),
        P("expert", None, None, "tensor"),
        P("expert", None, "tensor"),
        P(),
        P(),
    )
    out_specs = P(("dp", "expert"), "tensor")
    return jax.shard_map(local, mesh=mesh, in_specs=in_specs, out_specs=out_specs, check_vma=False)
```

time: 380 us -> 243 us (0.64)
  Pallas kernels: 0 us -> 154 us
  blocking collectives: 162 us -> 21.7 us
  waiting for transfers between devices: 130 us -> 0 us
  local copies, waits for them, and re-layouts: 38.2 us -> 18.7 us
  matrix products: 24.3 us -> 40.4 us
  between operations: 13.5 us -> 0.15 us
  starting transfers between devices: 6.04 us -> 0 us
    all_to_all x2 -> x0, blocking collectives: 162 us -> none  [the longest x1 81.7 us: local(): lax.all_to_all(outgoing, 'expert', split_axis=0, concat_axis=0, tiled=True)]
    pallas_call x0 -> x2, Pallas kernels: none -> 154 us  [the longest x1 81.7 us: gathered(): pl.pallas_call(functools.partial(scatter_kernel, zs, rows), out_shape=jax...]
    all_gather x2 -> x0, waiting for transfers between devices: 130 us -> none  [the longest x1 117 us: local(): piece = lax.all_gather(arrived, 'tensor', axis=2, tiled=True)]
    all_gather x0 -> x1, blocking collectives: none -> 21.7 us  [gathered(): lax.all_gather(weights_of(routes, gates, old_map, new_map).T, 'expert', a...]
    reshape x4 -> x0, local copies, waits for them, and re-layouts: 16.7 us -> none  [the longest x1 8.17 us: local(): flat_piece = piece.reshape(buffer_rows, piece.shape[2])]
    dot_general x4, matrix products: 24.3 us -> 40.4 us  [the longest x2 27.9 us: gathered(): jnp.dot(every[k], w_in[k * part:(k + 1) * part], preferred_element_type=j...]
    slice x1, local copies, waits for them, and re-layouts: 0.25 us -> 8.61 us  [gathered(): w_in[k * part:(k + 1) * part]]
    all_to_all x1 -> x0, local copies, waits for them, and re-layouts: 7.96 us -> none  [local(): lax.all_to_all(down_parts, 'tensor', split_axis=0, concat_axis=2, tiled=T...]
  transfers between devices with their start and end apart: 3 -> 0, of which waited for: 2 -> 0; matrix products, arithmetic and copies ran while one was open for 11% -> 0% of each run, Pallas kernels for 0% -> 0%
where the time goes in v1:
time: 243 us
  Pallas kernels  154 us (63%)
  matrix products  40.4 us (17%)
  blocking collectives  21.7 us (9%)
  local copies, waits for them, and re-layouts  18.7 us (8%)
  other arithmetic  7.9 us (3%)
    pallas_call x1, Pallas kernels, gathered(): pl.pallas_call(functools.partial(scatter_kernel, zs, rows), out_shape=jax...  81.7 us
    pallas_call x1, Pallas kernels, gathered(): pl.pallas_call(functools.partial(gather_kernel, zs, rows), out_shape=jax....  72.4 us
    dot_general x2, matrix products, gathered(): jnp.dot(every[k], w_in[k * part:(k + 1) * part], preferred_element_type=j...  27.9 us
    all_gather x1, blocking collectives, gathered(): lax.all_gather(weights_of(routes, gates, old_map, new_map).T, 'expert', a...  21.7 us
    dot_general x2, matrix products, gathered(): lax.dot_general(act, w_out[k], (((1,), (1,)), ((), ())), preferred_elemen...  12.5 us
    unnamed x14, local copies, waits for them, and re-layouts  10 us
    slice x1, local copies, waits for them, and re-layouts, gathered(): w_in[k * part:(k + 1) * part]  8.61 us
    another operation x1, other arithmetic, gathered(): jnp.stack([(share * lax.dot_general(act, w_out[k], (((1,), (1,)), ((), ()...  6.61 us

profile of v1, /device:TPU:0, one launch (start us, length us, event | category | flops | bytes accessed | tf_op | source)
XLA Modules:
  0.0 242.9 jit_solution(7901284191127230902)
XLA Ops:
  0.0 8.6 %fusion.16 = (bf16[1,2560,2,512]{3,2,1,0:T(2,128)(2,1)S(1)}, bf16[1,2560,2,512]{3,2,1,0:T(2,128)(2,1)S(1)}) fusion(bf16[1,5120,2,512]{3,2,1,0:T(2,128)(2,1)} %param.10), kind=kLoop, calls=%fused_computation.24 | loop fusion | bytes 20971520 | tf_op jit(solution)/shard_map/slice | solution.py:343
  8.6 4.0 %copy.19 = bf16[320,8,2,512]{3,1,2,0:T(8,128)(2,1)} copy(bf16[320,8,2,512]{3,2,1,0:T(2,128)(2,1)S(1)} %bitcast.32) | data formatting | bytes 10485760
  12.6 72.4 %gather_tokens.1 = bf16[2,1536,2560]{2,1,0:T(8,128)(2,1)} custom-call(bf16[96,2560]{1,0:T(8,128)(2,1)} %tok_ref.1), custom_call_target="tpu_custom_call" | custom-call | tf_op jit(solution)/shard_map/gather_tokens/pallas_call | solution.py:330
  85.0 0.0 copy-start
  85.0 14.0 %fusion.2 = f32[1536,1024]{1,0:T(8,128)} fusion(bf16[2560,1024]{1,0:T(8,128)(2,1)} %bitcast.34, bf16[2,1536,2560]{2,1,0:T(8,128)(2,1)} %gather_tokens.1), kind=kOutput, calls=%fused_computation.5 | convolution fusion | flops 8053063680 | bytes 19398656 | tf_op jit(solution)/shard_map/dot_general | solution.py:343
  99.0 4.0 %copy.18 = bf16[320,8,2,512]{3,1,2,0:T(8,128)(2,1)} copy(bf16[320,8,2,512]{3,2,1,0:T(2,128)(2,1)S(1)} %bitcast.31) | data formatting | bytes 10485760
  103.0 0.0 copy-done
  103.0 14.0 %fusion.8 = f32[1536,1024]{1,0:T(8,128)S(1)} fusion(f32[1536,1024]{1,0:T(8,128)} %fusion.2, bf16[2560,1024]{1,0:T(8,128)(2,1)} %bitcast.33, bf16[2,1536,2560]{2,1,0:T(8,128)(2,1)S(1)} %copy-done), kind=kOutput, calls=%fused_computation.11 | convolution fusion | flops 8054636544 | bytes 25690112 | tf_op jit(solution)/shard_map/dot_general | solution.py:343
  117.0 0.0 copy-start.3
  117.0 0.0 copy-start.4
  117.0 0.0 copy-start.1
  117.0 0.0 copy-start.2
  117.0 1.0 fusion.11
  118.1 0.0 copy-done.3
  118.1 0.0 copy-done.4
  118.1 0.2 select_reduce_fusion.2
  118.3 0.0 copy-done.1
  118.3 0.1 select_reduce_fusion.1
  118.3 0.0 copy-done.2
  118.4 21.7 %all-gather = f32[16,96,16]{1,2,0:T(8,128)S(1)} all-gather(f32[1,96,16]{1,2,0:T(8,128)S(1)} %bitcast.35), channel_id=1, replica_groups=mesh['expert'=16,'tensor'=2,'dp'=1] {'expert'}, dimensions={0}, use_global_device_ids=true | all-gather | bytes 104448 | tf_op jit(solution)/shard_map/all_gather | solution.py:326
  140.1 0.1 reshape.16
  140.2 6.3 %fusion.1 = bf16[1,1536,2560]{2,1,0:T(8,128)(2,1)S(1)} fusion(bf16[1536,512]{1,0:T(8,128)(2,1)S(1)} %fusion.11, f32[1536]{0:T(1024)S(1)} %dynamic-slice_reduce_fusion, bf16[1,5120,512]{2,1,0:T(8,128)(2,1)} %param.11), kind=kOutput, calls=%fused_computation.4 | convolution fusion | flops 4034396160 | bytes 12064768 | tf_op jit(solution)/shard_map/dot_general | solution.py:352
  146.5 6.3 %fusion = bf16[1,1536,2560]{2,1,0:T(8,128)(2,1)S(1)} fusion(bf16[1536,512]{1,0:T(8,128)(2,1)S(1)} %fusion.11, f32[1536]{0:T(1024)S(1)} %dynamic-slice_reduce_fusion, bf16[1,5120,512]{2,1,0:T(8,128)(2,1)} %param.11), kind=kOutput, calls=%fused_computation.3 | convolution fusion | flops 4034396160 | bytes 12064768 | tf_op jit(solution)/shard_map/dot_general | solution.py:352
  152.7 6.6 %pad_maximum_fusion.part_ref = bf16[2,1536,2560]{2,1,0:T(8,128)(2,1)} fusion(bf16[1,1536,2560]{2,1,0:T(8,128)(2,1)S(1)} %fusion.1, bf16[1,1536,2560]{2,1,0:T(8,128)(2,1)S(1)} %fusion), kind=kLoop, calls=%fused_computation | loop fusion | flops 7864320 | bytes 31457280 | tf_op jit(solution)/shard_map/stack | solution.py:348
  159.4 81.7 %scatter_sums.1 = bf16[96,2560]{1,0:T(8,128)(2,1)} custom-call(bf16[2,1536,2560]{2,1,0:T(8,128)(2,1)} %pad_maximum_fusion.part_ref), custom_call_target="tpu_custom_call" | custom-call | tf_op jit(solution)/shard_map/scatter_sums/pallas_call | solution.py:360
  241.0 1.8 copy.21
  (3 shorter events, 0.1 us)
Async XLA Ops:
  85.0 18.0 %copy-start = (bf16[2,1536,2560]{2,1,0:T(8,128)(2,1)S(1)}, bf16[2,1536,2560]{2,1,0:T(8,128)(2,1)}, u32[]{:S(2)}) copy-start(bf16[2,1536,2560]{2,1,0:T(8,128)(2,1)} %gather_tokens.1) | copy-start | bytes 47185924
  117.0 1.1 copy-start.3
  117.0 1.1 copy-start.4
  117.0 1.2 copy-start.1
  117.0 1.3 copy-start.2

commit v2 on v1

--- a/solution.py
+++ b/solution.py
@@ -36,15 +36,21 @@
 
 
 UP, DOWN, XL, YL, SIB = range(5)
-
-
-def gather_kernel(zs, rows, tok_ref, out_ref, local_sem, send_sem, recv_sem):
+TABLE = 2
+
+
+def gather_kernel(zs, rows, tok_ref, tab_ref, out_ref, all_ref, local_sem, send_sem, recv_sem):
     z, x, y, c = place(zs)
     half = rows // 2
+    part = tok_ref.shape[1]
     greet(zs, z, x, y, c)
 
     def slot(pz, px, py, pc, h):
-        return out_ref.at[py, pl.ds(((pz * 2 + px) * 2 + pc) * rows + h * half, half), :]
+        e = (pz * 2 + px) * 2 + pc
+        if h == TABLE:
+            return all_ref.at[e]
+        columns = pl.ds(pl.multiple_of(py * part, 128), part)
+        return out_ref.at[pl.ds(pl.multiple_of(e * rows + h * half, 16), half), columns]
 
     def index(pz, px, py):
         return (pz * 2 + px) * 2 + py
@@ -57,7 +63,9 @@
             device(z, x, 1 - y, c),
             device(z, x, y, 1 - c),
         )[link]
-        src = tok_ref.at[pl.ds(h * half, half), :] if own else slot(pz, px, py, c, h)
+        src = slot(pz, px, py, c, h)
+        if own:
+            src = tab_ref if h == TABLE else tok_ref.at[pl.ds(h * half, half), :]
         i = index(pz, px, py)
         return pltpu.make_async_remote_copy(
             src_ref=src,
@@ -89,6 +97,14 @@
         if not fv:
             act(copy(v, pz, px, py, h, own))
         act(copy(SIB, pz, px, py, h, own))
+        if h == 0 and not fv:
+            if not fu:
+                if d <= 0:
+                    pl.when(z < zs - 1)(lambda: act(copy(UP, pz, px, py, TABLE, own)))
+                if d >= 0:
+                    pl.when(z > 0)(lambda: act(copy(DOWN, pz, px, py, TABLE, own)))
+                act(copy(XL, pz, px, py, TABLE, own))
+            act(copy(SIB, pz, px, py, TABLE, own))
 
     events = [
         (d, fu, fv, h)
@@ -98,10 +114,14 @@
         for h in (0, 1)
     ]
     events.sort(key=lambda t: (abs(t[0]) + t[1] + t[2], t[2], t[1]))
+    e = (z * 2 + x) * 2 + c
+    columns = pl.ds(pl.multiple_of(y * part, 128), part)
     mine = pltpu.make_async_copy(
-        tok_ref, out_ref.at[y, pl.ds(((z * 2 + x) * 2 + c) * rows, rows), :], local_sem
-    )
+        tok_ref, out_ref.at[pl.ds(pl.multiple_of(e * rows, 16), rows), columns], local_sem.at[0]
+    )
+    listed = pltpu.make_async_copy(tab_ref, all_ref.at[e], local_sem.at[1])
     mine.start()
+    listed.start()
     for d, fu, fv, h in events:
 
         def step(d=d, fu=fu, fv=fv, h=h):
@@ -109,6 +129,8 @@
                 px = 1 - x if (fu if h == 0 else fv) else x
                 py = 1 - y if (fv if h == 0 else fu) else y
                 arrived(z + d, px, py, c, h)
+                if h == 0 and not fv:
+                    arrived(z + d, px, py, c, TABLE)
             hop(d, fu, fv, h, lambda k: k.start())
 
         if d == 0:
@@ -116,8 +138,10 @@
         else:
             pl.when((z + d >= 0) & (z + d < zs))(step)
     mine.wait()
+    listed.wait()
     for pz in range(zs):
         for px in range(2):
+            arrived(pz, px, y, 1 - c, TABLE)
             for py in range(2):
                 for h in range(2):
                     arrived(pz, px, py, 1 - c, h)
@@ -132,16 +156,25 @@
             pl.when((z + d >= 0) & (z + d < zs))(finish)
 
 
-def scatter_kernel(zs, rows, part_ref, out_ref, acc, rv, ru, rz, send_sem, sib_sem, v_sem, u_sem, z_sem):
+def scatter_kernel(
+    zs, rows, part_ref, out_ref, acc, held, rv, ru, rz, send_sem, own_sem, sib_sem, v_sem, u_sem, z_sem
+):
     z, x, y, c = place(zs)
     half = rows // 2
+    part = out_ref.shape[1]
     greet(zs, z, x, y, c)
 
     def index(pz, px, py):
         return (pz * 2 + px) * 2 + py
 
     def mine(pz, px, py, pc, h):
-        return part_ref.at[py, pl.ds(((pz * 2 + px) * 2 + pc) * rows + h * half, half), :]
+        first_row = ((pz * 2 + px) * 2 + pc) * rows + h * half
+        columns = pl.ds(pl.multiple_of(py * part, 128), part)
+        return part_ref.at[pl.ds(pl.multiple_of(first_row, 16), half), columns]
+
+    def own_copy(pz, px, py, h):
+        i = index(pz, px, py)
+        return pltpu.make_async_copy(mine(pz, px, py, c, h), held.at[i, h], own_sem.at[i, h])
 
     def spot(d, fu, fv, h):
         return z + d, (1 - x if (fu if h == 0 else fv) else x), (1 - y if (fv if h == 0 else fu) else y)
@@ -225,6 +258,7 @@
             for fu, fv in pairs:
                 for h in (0, 1):
                     when_there(d, lambda: sib_copy(*spot(d, fu, fv, h), h).start())
+                    when_there(d, lambda: own_copy(*spot(d, fu, fv, h), h).start())
 
     def stage0(ds):
         for d in ds:
@@ -235,7 +269,8 @@
                         pz, px, py = spot(d, fu, fv, h)
                         i = index(pz, px, py)
                         landed(acc.at[i, h], sib_sem.at[i, h])
-                        add(acc.at[i, h], acc.at[i, h], mine(pz, px, py, c, h))
+                        own_copy(pz, px, py, h).wait()
+                        add(acc.at[i, h], acc.at[i, h], held.at[i, h])
                         if fv:
                             v_copy(d, fu, h).start()
 
@@ -323,51 +358,47 @@
     _, width, _, hidden = gate_up.shape
     dma = pltpu.SemaphoreType.DMA
     mine = lax.axis_index("expert")
-    table = lax.all_gather(
-        weights_of(routes, gates, old_map, new_map).T, "expert", axis=1, tiled=True
-    )
-    share = lax.dynamic_index_in_dim(table, mine, 0, keepdims=False)[:, None]
-    every = pl.pallas_call(
+    lanes = -(-rows // 128) * 128
+    table = jnp.pad(weights_of(routes, gates, old_map, new_map).T, ((0, 0), (0, lanes - rows)))
+    every, tables = pl.pallas_call(
         functools.partial(gather_kernel, zs, rows),
-        out_shape=jax.ShapeDtypeStruct((tensors, experts * rows, part), tokens.dtype),
-        in_specs=[pl.BlockSpec(memory_space=pl.ANY)],
-        out_specs=pl.BlockSpec(memory_space=pl.ANY),
-        scratch_shapes=[dma, dma((5, zs * 4, 2)), dma((2, zs * 4, 2))],
+        out_shape=(
+            jax.ShapeDtypeStruct((experts * rows, tensors * part), tokens.dtype),
+            jax.ShapeDtypeStruct((experts, experts, lanes), jnp.float32),
+        ),
+        in_specs=[pl.BlockSpec(memory_space=pl.ANY)] * 2,
+        out_specs=[pl.BlockSpec(memory_space=pl.ANY)] * 2,
+        scratch_shapes=[dma((2,)), dma((5, zs * 4, 3)), dma((2, zs * 4, 3))],
         compiler_params=pltpu.CompilerParams(
             collective_id=0, has_side_effects=True, vmem_limit_bytes=VMEM_BUDGET
         ),
         name="gather_tokens",
-    )(tokens)
-    w_in = gate_up.reshape(width, 2 * hidden)
-    projected = sum(
-        jnp.dot(every[k], w_in[k * part : (k + 1) * part], preferred_element_type=jnp.float32)
-        for k in range(tensors)
-    )
-    act = (jax.nn.silu(projected[:, :hidden]) * projected[:, hidden:]).astype(jnp.bfloat16)
-    w_out = down_weight.reshape(tensors, part, hidden)
-    partial = jnp.stack(
-        [
-            (
-                share
-                * lax.dot_general(
-                    act, w_out[k], (((1,), (1,)), ((), ())), preferred_element_type=jnp.float32
-                )
-            ).astype(jnp.bfloat16)
-            for k in range(tensors)
-        ]
-    )
+    )(tokens, table)
+    share = lax.dynamic_index_in_dim(tables, mine, 1, keepdims=False)[:, :rows].reshape(-1, 1)
+    projected = jnp.dot(
+        every, gate_up.reshape(width, 2 * hidden), preferred_element_type=jnp.float32
+    )
+    gate, up = projected[:, :hidden], projected[:, hidden:]
+    act = (jax.nn.silu(gate) * up).astype(jnp.bfloat16)
+    w_out = down_weight.reshape(width, hidden)
+    partial = share * lax.dot_general(
+        act, w_out, (((1,), (1,)), ((), ())), preferred_element_type=jnp.float32
+    )
+    partial = partial.astype(jnp.bfloat16)
     half = rows // 2
     return pl.pallas_call(
         functools.partial(scatter_kernel, zs, rows),
         out_shape=jax.ShapeDtypeStruct((rows, part), jnp.bfloat16),
-        in_specs=[pl.BlockSpec(memory_space=pltpu.VMEM)],
+        in_specs=[pl.BlockSpec(memory_space=pl.ANY)],
         out_specs=pl.BlockSpec(memory_space=pltpu.VMEM),
         scratch_shapes=[
+            pltpu.VMEM((zs * 4, 2, half, part), jnp.bfloat16),
             pltpu.VMEM((zs * 4, 2, half, part), jnp.bfloat16),
             pltpu.VMEM((zs * 2, 2, half, part), jnp.bfloat16),
             pltpu.VMEM((zs, 2, half, part), jnp.bfloat16),
             pltpu.VMEM((2, zs, 2, half, part), jnp.bfloat16),
             dma((4, zs * 4, 2)),
+            dma((zs * 4, 2)),
             dma((zs * 4, 2)),
             dma((zs * 2, 2)),
             dma((zs, 2)),

time: 243 us -> 209 us (0.86)
  blocking collectives: 21.7 us -> 0 us
  other arithmetic: 7.9 us -> 2.33 us
  local copies, waits for them, and re-layouts: 18.7 us -> 14.7 us
    all_gather x1 -> x0, blocking collectives: 21.7 us -> none  [gathered(): lax.all_gather(weights_of(routes, gates, old_map, new_map).T, 'expert', a...]
    slice x1 -> x0, local copies, waits for them, and re-layouts: 8.61 us -> none  [gathered(): w_in[k * part:(k + 1) * part]]
    another operation x1 -> x0, other arithmetic: 6.61 us -> none  [gathered(): jnp.stack([(share * lax.dot_general(act, w_out[k], (((1,), (1,)), ((), ()...]
    unnamed x14 -> x2, local copies, waits for them, and re-layouts: 10 us -> 13.1 us
    dot_general x4 -> x2, matrix products: 40.4 us -> 38.8 us  [the longest x1 23.6 us: gathered(): jnp.dot(every, gate_up.reshape(width, 2 * hidden), preferred_element_type...]
where the time goes in v2:
time: 209 us
  Pallas kernels  153 us (73%)
  matrix products  38.8 us (19%)
  local copies, waits for them, and re-layouts  14.7 us (7%)
  other arithmetic  2.33 us (1%)
    pallas_call x1, Pallas kernels, gathered(): pl.pallas_call(functools.partial(scatter_kernel, zs, rows), out_shape=jax...  79.6 us
    pallas_call x1, Pallas kernels, gathered(): pl.pallas_call(functools.partial(gather_kernel, zs, rows), out_shape=(jax...  73.7 us
    dot_general x1, matrix products, gathered(): jnp.dot(every, gate_up.reshape(width, 2 * hidden), preferred_element_type...  23.6 us
    dot_general x1, matrix products, gathered(): lax.dot_general(act, w_out, (((1,), (1,)), ((), ())), preferred_element_t...  15.3 us
    unnamed x2, local copies, waits for them, and re-layouts  13.1 us

profile of v2, /device:TPU:0, one launch (start us, length us, event | category | flops | bytes accessed | tf_op | source)
XLA Modules:
  0.0 209.1 jit_solution(7586636305761635920)
XLA Ops:
  0.0 0.9 select_reduce_fusion.2
  0.9 0.8 select_reduce_fusion.1
  1.6 0.7 select_reduce_fusion
  2.3 0.6 pad.4.tab_ref
  2.9 73.7 %gather_tokens.1 = (bf16[1536,5120]{1,0:T(8,128)(2,1)}, f32[16,16,128]{2,1,0:T(8,128)}) custom-call(bf16[96,2560]{1,0:T(8,128)(2,1)} %tok_ref.1, f32[16,128]{1,0:T(8,128)} %pad.4.tab_ref), custom_call_target="tpu_custom_call" | custom-call | tf_op jit(solution)/shard_map/gather_tokens/pallas_call | solution.py:363
  76.6 0.9 constant_dynamic-slice_fusion
  77.5 0.1 mul.17
  77.6 11.3 %copy.10 = bf16[640,8,2,512]{3,1,2,0:T(8,128)(2,1)} copy(bf16[640,8,2,512]{3,2,1,0:T(2,128)(2,1)} %bitcast.11) | data formatting | bytes 20971520
  88.8 23.6 %fusion.5 = f32[1536,1024]{1,0:T(8,128)} fusion(bf16[1536,5120]{1,0:T(8,128)(2,1)} %get-tuple-element.8, bf16[5120,1024]{1,0:T(8,128)(2,1)} %bitcast.12), kind=kOutput, calls=%fused_computation.12 | convolution fusion | flops 16106127360 | bytes 32505856 | tf_op jit(solution)/shard_map/dot_general | solution.py:378
  112.4 15.3 %multiply_convert_fusion.part_ref = bf16[1536,5120]{1,0:T(8,128)(2,1)} fusion(f32[1536]{0:T(1024)S(1)} %mul.17, bf16[1,5120,512]{2,1,0:T(8,128)(2,1)} %param.11, f32[1536,1024]{1,0:T(8,128)} %fusion.5), kind=kOutput, calls=%fused_computation | convolution fusion | flops 8073510912 | bytes 27269120 | tf_op jit(solution)/shard_map/dot_general | solution.py:384
  127.7 79.6 %scatter_sums.1 = bf16[96,2560]{1,0:T(8,128)(2,1)} custom-call(bf16[1536,5120]{1,0:T(8,128)(2,1)} %multiply_convert_fusion.part_ref), custom_call_target="tpu_custom_call" | custom-call | tf_op jit(solution)/shard_map/scatter_sums/pallas_call | solution.py:389
  207.3 1.8 copy.12
